TPU v7x, 256 devices: a whole 4x4x8 slice. The times are simulated.
256 devices in a mesh: kx: 4 (over x), ky: 4 (over z_hi), kz: 16 (over z_lo, y, core).
Axes of the slice: x: 4, y: 4, z: 8 (z_hi: 4, z_lo: 2; z = z_hi * 2 + z_lo), core: 2. Of those that a mesh axis runs over, the one named last changes fastest.
Arguments:
- orbitals: bfloat16 [16, 16, 16, 1024, 128], P('kx', 'ky', 'kz'), may hold values from -6 to 6
- kernel: bfloat16 [256, 2, 1024, 1024], P(('kx', 'ky', 'kz')), may hold values from -0.00015258789 to 0.00015258789
- plan: int32 [2, 2, 256], replicated, may hold values from 0 to 15, as said below
- occupation: int32 [16, 16, 16, 64], replicated, may hold values 0 or 1
Outputs:
- exchange_blocks: float32 [16, 16, 16, 64, 128], P('kx', 'ky', 'kz')
Inputs may be any that keep to these rules, and one draw needn't show every extreme that they name: `plan`: entry [r, 0, e] is the slot, in device e's block of 4 x 4 x 1 k-points, of the k-point that e sends as k in round r, and [r, 1, e] the slot of the one it sends as p. For every owner, k minus p is the same momentum transfer on the periodic k-mesh in every round.
All inputs are finite; a program needn't handle non-finite values.
Results may differ from a plain program's by a relative error of at most 0.004.
Values may be sent and summed in bfloat16 or wider, within the bound.
A program may use at most 128 MiB of HBM per device.

v0:
```python
import jax
import jax.numpy as jnp
from jax import lax
from jax.sharding import PartitionSpec as P


def shifted(block, axis, distance):
    devices = range(lax.axis_size(axis))
    route = [((i - distance) % len(devices), i) for i in devices]
    return lax.ppermute(block, axis, route)


def hop_shifts(turn_number, mesh_counts):
    forward = (
        (turn_number + 1) % mesh_counts[0],
        (2 * turn_number + 1) % mesh_counts[1],
        (3 * turn_number + 1) % mesh_counts[2],
    )
    partner = (forward[0], forward[1], (forward[2] - mesh_counts[2] // 2) % mesh_counts[2])
    return (forward, partner)


def negated(shift, mesh_counts):
    return (-shift[0] % mesh_counts[0], -shift[1] % mesh_counts[1], -shift[2] % mesh_counts[2])


def global_points(plan, turn_number, column, shift, owner_coords, mesh_counts, cell_counts):
    sender_first = (owner_coords[0] - shift[0]) % mesh_counts[0]
    sender_second = (owner_coords[1] - shift[1]) % mesh_counts[1]
    sender_third = (owner_coords[2] - shift[2]) % mesh_counts[2]
    linear = (sender_first * mesh_counts[1] + sender_second) * mesh_counts[2] + sender_third
    slot_index = plan[turn_number, column, linear]
    cell_first = slot_index // (cell_counts[1] * cell_counts[2])
    cell_second = slot_index // cell_counts[2] % cell_counts[1]
    cell_third = slot_index % cell_counts[2]
    return (
        sender_first * cell_counts[0] + cell_first,
        sender_second * cell_counts[1] + cell_second,
        sender_third * cell_counts[2] + cell_third,
    )


def density_product(orbital, occupied):
    bands = orbital.shape[1] // 2
    weights = jnp.concatenate([occupied, occupied]).astype(orbital.dtype)
    masked = orbital * weights[None, :]
    swapped = jnp.concatenate([-orbital[:, bands:], orbital[:, :bands]], axis=1)
    density_real = jnp.dot(masked, orbital.T, preferred_element_type=jnp.float32)
    density_imag = jnp.dot(masked, swapped.T, preferred_element_type=jnp.float32)
    return (density_real, density_imag)


def kernel_hadamard(kernel_real, kernel_imag, density_real, density_imag, conjugate_sign):
    weight_real = kernel_real.astype(jnp.float32)
    weight_imag = kernel_imag.astype(jnp.float32) * conjugate_sign
    hadamard_real = weight_real * density_real - weight_imag * density_imag
    hadamard_imag = weight_real * density_imag + weight_imag * density_real
    return jnp.concatenate([hadamard_real, hadamard_imag], axis=1).astype(jnp.bfloat16)


def exchange_block(stacked, orbital):
    bands = orbital.shape[1] // 2
    real_part = orbital[:, :bands]
    imag_part = orbital[:, bands:]
    blocked = jnp.concatenate([orbital, jnp.concatenate([-imag_part, real_part], axis=1)], axis=0)
    mixture = jnp.dot(stacked, blocked, preferred_element_type=jnp.float32).astype(jnp.bfloat16)
    gram_matrix = lax.dot_general(
        orbital, mixture, (((0,), (0,)), ((), ())), preferred_element_type=jnp.float32
    )
    result_real = -(gram_matrix[:bands, :bands] + gram_matrix[bands:, bands:])
    result_imag = -(gram_matrix[:bands, bands:] - gram_matrix[bands:, :bands])
    return jnp.concatenate([result_real, result_imag], axis=1)


def pair_blocks(
    kernel_real, kernel_imag, orbital_first, occupied_first, orbital_second, occupied_second
):
    second_real, second_imag = density_product(orbital_second, occupied_second)
    first_block = exchange_block(
        kernel_hadamard(kernel_real, kernel_imag, second_real, second_imag, 1.0), orbital_first
    )
    first_real, first_imag = density_product(orbital_first, occupied_first)
    second_block = exchange_block(
        kernel_hadamard(kernel_real, kernel_imag, first_real, first_imag, -1.0), orbital_second
    )
    return (first_block, second_block)


def orbit_hops(payload, amounts):
    payload = shifted(payload, "kx", amounts[0])
    payload = shifted(payload, "ky", amounts[1])
    payload = shifted(payload, "kz", amounts[2])
    return payload


def return_hops(payload, amounts):
    payload = shifted(payload, "kx", amounts[0])
    payload = shifted(payload, "ky", amounts[1])
    payload = shifted(payload, "kz", amounts[2])
    return payload


def on_device(orbitals, kernel, plan, occupation):
    mesh_counts = (lax.axis_size("kx"), lax.axis_size("ky"), lax.axis_size("kz"))
    places = (lax.axis_index("kx"), lax.axis_index("ky"), lax.axis_index("kz"))
    own_linear = (places[0] * mesh_counts[1] + places[1]) * mesh_counts[2] + places[2]
    cell_counts = orbitals.shape[:3]
    point_total = cell_counts[0] * cell_counts[1] * cell_counts[2]
    local_orbitals = orbitals.reshape(point_total, orbitals.shape[3], orbitals.shape[4])
    bands = orbitals.shape[4] // 2
    kernel_real = kernel[0, 0]
    kernel_imag = kernel[0, 1]
    slot_numbers = jnp.arange(point_total, dtype=jnp.int32)
    totals = jnp.zeros((point_total, bands, 2 * bands), jnp.float32)
    for turn_number in range(plan.shape[0]):
        forward, partner = hop_shifts(turn_number, mesh_counts)
        first_slot = plan[turn_number, 0, own_linear]
        second_slot = plan[turn_number, 1, own_linear]
        first_send = lax.dynamic_index_in_dim(local_orbitals, first_slot, 0, keepdims=False)
        second_send = lax.dynamic_index_in_dim(local_orbitals, second_slot, 0, keepdims=False)
        first_orbital = orbit_hops(first_send, forward)
        second_orbital = orbit_hops(second_send, partner)
        first_point = global_points(plan, turn_number, 0, forward, places, mesh_counts, cell_counts)
        second_point = global_points(
            plan, turn_number, 1, partner, places, mesh_counts, cell_counts
        )
        first_occupied = occupation[first_point[0], first_point[1], first_point[2]]
        second_occupied = occupation[second_point[0], second_point[1], second_point[2]]
        first_block, second_block = pair_blocks(
            kernel_real, kernel_imag, first_orbital, first_occupied, second_orbital, second_occupied
        )
        returned_first = return_hops(first_block, negated(forward, mesh_counts))
        returned_second = return_hops(second_block, negated(partner, mesh_counts))
        first_pick = (slot_numbers == first_slot).astype(jnp.float32)[:, None, None]
        second_pick = (slot_numbers == second_slot).astype(jnp.float32)[:, None, None]
        totals = totals + first_pick * returned_first[None] + second_pick * returned_second[None]
    return totals.reshape(cell_counts[0], cell_counts[1], cell_counts[2], bands, 2 * bands)


def solution(mesh):
    placed = (P("kx", "ky", "kz", None, None), P(("kx", "ky", "kz"), None, None, None), P(), P())
    return jax.shard_map(
        on_device,
        mesh=mesh,
        in_specs=placed,
        out_specs=P("kx", "ky", "kz", None, None),
        check_vma=False,
    )
```

profile of v0, /device:TPU:32, one launch (start us, length us, event | category | flops | bytes accessed | tf_op | source)
XLA Modules:
  0.0 150.5 jit_solution(3487245310767447022)
XLA Ops:
  10.5 3.1 %collective-permute-start.12 = (bf16[1024,128]{1,0:T(8,128)(2,1)S(1)}, bf16[1024,128]{1,0:T(8,128)(2,1)S(1)}, u32[]{:S(2)}, u32[]{:S(2)}) collective-permute-start(bf16[1024,128]{1,0:T(8,128)(2,1)S(1)} %get-tuple-element.21), channel_id=1, source_target_pairs={{128,0},{192,64},{0,128},{64,192},{129,1},{193,65},{1,129},{65,193... | collective-permute-start | bytes 786440 | tf_op jit(solution)/shard_map/ppermute | solution.py:10
  27.3 5.5 %collective-permute-start.13 = (bf16[1024,128]{1,0:T(8,128)(2,1)S(1)}, bf16[1024,128]{1,0:T(8,128)(2,1)}, u32[]{:S(2)}, u32[]{:S(2)}) collective-permute-start(bf16[1024,128]{1,0:T(8,128)(2,1)S(1)} %collective-permute-done.12), channel_id=1, source_target_pairs={{16,0},{32,16},{48,32},{0,48},{17,1},{33,17},{49,33},{1,49},{18,2}... | collective-permute-start | bytes 786440 | tf_op jit(solution)/shard_map/ppermute | solution.py:10
  32.8 4.7 %fusion.172 = (bf16[1,1,1024,1024]{3,2,1,0:T(8,128)(2,1)}, bf16[1,1,1024,1024]{3,2,1,0:T(8,128)(2,1)}) fusion(bf16[1,2,1024,1024]{3,2,1,0:T(8,128)(2,1)} %param.5), kind=kLoop, calls=%fused_computation.183 | loop fusion | bytes 8388608 | tf_op jit(solution)/shard_map/slice | solution.py:111
  40.6 4.5 %collective-permute-done.13 = bf16[1024,128]{1,0:T(8,128)(2,1)} collective-permute-done((bf16[1024,128]{1,0:T(8,128)(2,1)S(1)}, bf16[1024,128]{1,0:T(8,128)(2,1)}, u32[]{:S(2)}, u32[]{:S(2)}) %collective-permute-start.13) | collective-permute-done | bytes 262176 | tf_op jit(solution)/shard_map/ppermute | solution.py:10
  45.0 3.2 %collective-permute-start.14 = (bf16[1024,128]{1,0:T(8,128)(2,1)}, bf16[1024,128]{1,0:T(8,128)(2,1)S(1)}, u32[]{:S(2)}, u32[]{:S(2)}) collective-permute-start(bf16[1024,128]{1,0:T(8,128)(2,1)} %collective-permute-done.13), channel_id=1, source_target_pairs={{12,0},{13,1},{14,2},{15,3},{0,4},{1,5},{2,6},{3,7},{4,8},{5,9},{6... | collective-permute-start | bytes 786440 | tf_op jit(solution)/shard_map/ppermute | solution.py:10
  48.9 2.9 %copy.7 = bf16[1,1,1024,1024]{2,3,1,0:T(8,128)(2,1)S(1)} copy(bf16[1,1,1024,1024]{3,2,1,0:T(8,128)(2,1)} %get-tuple-element.23) | data formatting | bytes 4194304
  51.8 3.9 %copy.8 = bf16[1,1,1024,1024]{2,3,1,0:T(8,128)(2,1)} copy(bf16[1,1,1024,1024]{3,2,1,0:T(8,128)(2,1)} %get-tuple-element.24) | data formatting | bytes 4194304
  58.8 4.5 %collective-permute-done.4 = bf16[1024,128]{1,0:T(8,128)(2,1)} collective-permute-done((bf16[1024,128]{1,0:T(8,128)(2,1)S(1)}, bf16[1024,128]{1,0:T(8,128)(2,1)}, u32[]{:S(2)}, u32[]{:S(2)}) %collective-permute-start.4) | collective-permute-done | bytes 262176 | tf_op jit(solution)/shard_map/ppermute | solution.py:10
  63.3 10.0 %collective-permute-done.14 = bf16[1024,128]{1,0:T(8,128)(2,1)S(1)} collective-permute-done((bf16[1024,128]{1,0:T(8,128)(2,1)}, bf16[1024,128]{1,0:T(8,128)(2,1)S(1)}, u32[]{:S(2)}, u32[]{:S(2)}) %collective-permute-start.14) | collective-permute-done | bytes 262176 | tf_op jit(solution)/shard_map/ppermute | solution.py:10
  73.3 2.7 %fusion.102 = f32[1024,1024]{0,1:T(8,128)} fusion(bf16[1024,128]{1,0:T(8,128)(2,1)S(1)} %collective-permute-done.14, bf16[128]{0:T(256)(128)(2,1)S(1)} %get-tuple-element.56), kind=kOutput, calls=%fused_computation.80 | convolution fusion | flops 268566528 | bytes 4456704 | tf_op jit(solution)/shard_map/dot_general | solution.py:48
  76.0 2.7 %fusion.106 = f32[1024,1024]{0,1:T(8,128)} fusion(bf16[1024,128]{1,0:T(8,128)(2,1)S(1)} %collective-permute-done.17, bf16[128]{0:T(256)(128)(2,1)S(1)} %get-tuple-element.55), kind=kOutput, calls=%fused_computation.84 | convolution fusion | flops 268566528 | bytes 4456704 | tf_op jit(solution)/shard_map/dot_general | solution.py:48
  78.9 2.8 %fusion.110 = f32[1024,1024]{0,1:T(8,128)} fusion(bf16[1024,128]{1,0:T(8,128)(2,1)S(1)} %collective-permute-done.2, bf16[128]{0:T(256)(128)(2,1)S(1)} %get-tuple-element.54), kind=kOutput, calls=%fused_computation.88 | convolution fusion | flops 268566528 | bytes 4456704 | tf_op jit(solution)/shard_map/dot_general | solution.py:48
  85.5 2.8 %fusion.100 = f32[1024,1024]{0,1:T(8,128)} fusion(bf16[1024,128]{1,0:T(8,128)(2,1)S(1)} %collective-permute-done.14, bf16[1024,64]{1,0:T(8,128)(2,1)S(1)} %get-tuple-element.36, bf16[1024,64]{1,0:T(8,128)(2,1)S(1)} %get-tuple-element.35, bf16[128]{0:T(256)(128)(2,1)S(1)} %get-tuple-element.56), kind=kOutput, calls=%fused_computation.78 | convolution fusion | flops 269090816 | bytes 4718848 | tf_op jit(solution)/shard_map/dot_general | solution.py:49
  88.3 2.7 %fusion.104 = f32[1024,1024]{0,1:T(8,128)} fusion(bf16[1024,128]{1,0:T(8,128)(2,1)S(1)} %collective-permute-done.17, bf16[1024,64]{1,0:T(8,128)(2,1)S(1)} %get-tuple-element.34, bf16[1024,64]{1,0:T(8,128)(2,1)S(1)} %get-tuple-element.33, bf16[128]{0:T(256)(128)(2,1)S(1)} %get-tuple-element.55), kind=kOutput, calls=%fused_computation.82 | convolution fusion | flops 269090816 | bytes 4718848 | tf_op jit(solution)/shard_map/dot_general | solution.py:49
  91.0 2.8 %fusion.108 = f32[1024,1024]{0,1:T(8,128)} fusion(bf16[1024,128]{1,0:T(8,128)(2,1)S(1)} %collective-permute-done.2, bf16[1024,64]{1,0:T(8,128)(2,1)S(1)} %get-tuple-element.32, bf16[1024,64]{1,0:T(8,128)(2,1)S(1)} %get-tuple-element.31, bf16[128]{0:T(256)(128)(2,1)S(1)} %get-tuple-element.54), kind=kOutput, calls=%fused_computation.86 | convolution fusion | flops 269090816 | bytes 4718848 | tf_op jit(solution)/shard_map/dot_general | solution.py:49
  93.8 15.9 %fusion.13 = (bf16[1024,1024]{0,1:T(8,128)(2,1)}, bf16[1024,1024]{0,1:T(8,128)(2,1)}, bf16[1024,1024]{0,1:T(8,128)(2,1)}, bf16[1024,1024]{0,1:T(8,128)(2,1)}, bf...) fusion(f32[1024,1024]{0,1:T(8,128)} %fusion.114, ...), kind=kOutput, calls=%fused_computation.26 | convolution fusion | flops 305790976 | bytes 50856192 | tf_op jit(solution)/shard_map/dot_general | solution.py:49
  109.7 4.0 %fusion.49 = f32[128,128]{1,0:T(8,128)S(1)} fusion(bf16[1024,128]{1,0:T(8,128)(2,1)S(1)} %collective-permute-done.2, bf16[1024,1024]{0,1:T(8,128)(2,1)} %get-tuple-element.6, bf16[1024,1024]{0,1:T(8,128)(2,1)} %get-tuple-element.5, bf16[1024,64]{1,0:T(8,128)(2,1)} %copy-done.9, bf16[1024,64]{1,0:T(8,128)(2,1)} %copy-done.8), kind=kOutput, calls=%fused_computation.53 | convolution fusion | flops 580517888 | bytes 4784128 | tf_op jit(solution)/shard_map/dot_general | solution.py:67
  115.8 3.2 %fusion.52 = f32[128,128]{1,0:T(8,128)S(1)} fusion(bf16[1024,128]{1,0:T(8,128)(2,1)S(1)} %collective-permute-done.5, bf16[1024,1024]{0,1:T(8,128)(2,1)S(1)} %copy-done.1, bf16[1024,1024]{0,1:T(8,128)(2,1)} %get-tuple-element.16, bf16[1024,64]{1,0:T(8,128)(2,1)} %get-tuple-element.30, bf16[1024,64]{1,0:T(8,128)(2,1)S(1)} %get-tuple-element.29), kind=kOutput, calls=%fused_computation.54 | convolution fusion | flops 580517888 | bytes 4784128 | tf_op jit(solution)/shard_map/dot_general | solution.py:67
  119.8 4.0 %fusion.55 = f32[128,128]{1,0:T(8,128)S(1)} fusion(bf16[1024,128]{1,0:T(8,128)(2,1)S(1)} %collective-permute-done.14, bf16[1024,1024]{0,1:T(8,128)(2,1)} %get-tuple-element.13, bf16[1024,1024]{0,1:T(8,128)(2,1)} %get-tuple-element.14, bf16[1024,64]{1,0:T(8,128)(2,1)} %copy-done.7, bf16[1024,64]{1,0:T(8,128)(2,1)} %copy-done.6), kind=kOutput, calls=%fused_computation.55 | convolution fusion | flops 580517888 | bytes 4784128 | tf_op jit(solution)/shard_map/dot_general | solution.py:67
  125.9 3.2 %fusion.58 = f32[128,128]{1,0:T(8,128)S(1)} fusion(bf16[1024,128]{1,0:T(8,128)(2,1)S(1)} %collective-permute-done.17, bf16[1024,1024]{0,1:T(8,128)(2,1)S(1)} %copy-done, bf16[1024,1024]{0,1:T(8,128)(2,1)} %get-tuple-element.18, bf16[1024,64]{1,0:T(8,128)(2,1)S(1)} %copy-done.5, bf16[1024,64]{1,0:T(8,128)(2,1)S(1)} %copy-done.3), kind=kOutput, calls=%fused_computation.56 | convolution fusion | flops 580517888 | bytes 4784128 | tf_op jit(solution)/shard_map/dot_general | solution.py:67
  130.9 3.1 %collective-permute-start.7 = (f32[64,128]{1,0:T(8,128)S(1)}, f32[64,128]{1,0:T(8,128)S(1)}, u32[]{:S(2)}, u32[]{:S(2)}) collective-permute-start(f32[64,128]{1,0:T(8,128)S(1)} %collective-permute-done.6), channel_id=1, source_target_pairs={{16,0},{32,16},{48,32},{0,48},{17,1},{33,17},{49,33},{1,49},{18,2}... | collective-permute-start | bytes 98312 | tf_op jit(solution)/shard_map/ppermute | solution.py:10
  134.2 2.7 %collective-permute-start.19 = (f32[64,128]{1,0:T(8,128)S(1)}, f32[64,128]{1,0:T(8,128)S(1)}, u32[]{:S(2)}, u32[]{:S(2)}) collective-permute-start(f32[64,128]{1,0:T(8,128)S(1)} %collective-permute-done.18), channel_id=1, source_target_pairs={{48,0},{0,16},{16,32},{32,48},{49,1},{1,17},{17,33},{33,49},{50,2}... | collective-permute-start | bytes 98312 | tf_op jit(solution)/shard_map/ppermute | solution.py:10
  140.2 2.9 %collective-permute-start.20 = (f32[64,128]{1,0:T(8,128)S(1)}, f32[64,128]{1,0:T(8,128)S(1)}, u32[]{:S(2)}, u32[]{:S(2)}) collective-permute-start(f32[64,128]{1,0:T(8,128)S(1)} %collective-permute-done.19), channel_id=1, source_target_pairs={{4,0},{5,1},{6,2},{7,3},{8,4},{9,5},{10,6},{11,7},{12,8},{13,9},{1... | collective-permute-start | bytes 98312 | tf_op jit(solution)/shard_map/ppermute | solution.py:10
  145.9 3.6 %collective-permute-done.23 = f32[64,128]{1,0:T(8,128)S(1)} collective-permute-done((f32[64,128]{1,0:T(8,128)S(1)}, f32[64,128]{1,0:T(8,128)S(1)}, u32[]{:S(2)}, u32[]{:S(2)}) %collective-permute-start.23) | collective-permute-done | bytes 32800 | tf_op jit(solution)/shard_map/ppermute | solution.py:10
  (79 shorter events, 30.9 us)
Async XLA Ops:
  10.5 16.9 %collective-permute-start.12 = (bf16[1024,128]{1,0:T(8,128)(2,1)S(1)}, bf16[1024,128]{1,0:T(8,128)(2,1)S(1)}, u32[]{:S(2)}, u32[]{:S(2)}) collective-permute-start(bf16[1024,128]{1,0:T(8,128)(2,1)S(1)} %get-tuple-element.21), channel_id=1, source_target_pairs={{128,0},{192,64},{0,128},{64,192},{129,1},{193,65},{1,129},{65,193... | collective-permute-start | bytes 786440 | tf_op jit(solution)/shard_map/ppermute | solution.py:10
  13.6 24.0 %collective-permute-start.15 = (bf16[1024,128]{1,0:T(8,128)(2,1)S(1)}, bf16[1024,128]{1,0:T(8,128)(2,1)S(1)}, u32[]{:S(2)}, u32[]{:S(2)}) collective-permute-start(bf16[1024,128]{1,0:T(8,128)(2,1)S(1)} %get-tuple-element.20), channel_id=1, source_target_pairs={{128,0},{192,64},{0,128},{64,192},{129,1},{193,65},{1,129},{65,193... | collective-permute-start | bytes 786440 | tf_op jit(solution)/shard_map/ppermute | solution.py:10
  14.1 24.9 %collective-permute-start = (bf16[1024,128]{1,0:T(8,128)(2,1)S(1)}, bf16[1024,128]{1,0:T(8,128)(2,1)S(1)}, u32[]{:S(2)}, u32[]{:S(2)}) collective-permute-start(bf16[1024,128]{1,0:T(8,128)(2,1)S(1)} %get-tuple-element.19), channel_id=1, source_target_pairs={{192,0},{0,64},{64,128},{128,192},{193,1},{1,65},{65,129},{129,193... | collective-permute-start | bytes 786440 | tf_op jit(solution)/shard_map/ppermute | solution.py:10
  15.6 24.9 %collective-permute-start.3 = (bf16[1024,128]{1,0:T(8,128)(2,1)S(1)}, bf16[1024,128]{1,0:T(8,128)(2,1)S(1)}, u32[]{:S(2)}, u32[]{:S(2)}) collective-permute-start(bf16[1024,128]{1,0:T(8,128)(2,1)S(1)} %get-tuple-element.22), channel_id=1, source_target_pairs={{192,0},{0,64},{64,128},{128,192},{193,1},{1,65},{65,129},{129,193... | collective-permute-start | bytes 786440 | tf_op jit(solution)/shard_map/ppermute | solution.py:10
  27.3 17.7 %collective-permute-start.13 = (bf16[1024,128]{1,0:T(8,128)(2,1)S(1)}, bf16[1024,128]{1,0:T(8,128)(2,1)}, u32[]{:S(2)}, u32[]{:S(2)}) collective-permute-start(bf16[1024,128]{1,0:T(8,128)(2,1)S(1)} %collective-permute-done.12), channel_id=1, source_target_pairs={{16,0},{32,16},{48,32},{0,48},{17,1},{33,17},{49,33},{1,49},{18,2}... | collective-permute-start | bytes 786440 | tf_op jit(solution)/shard_map/ppermute | solution.py:10
  37.5 18.3 %collective-permute-start.16 = (bf16[1024,128]{1,0:T(8,128)(2,1)S(1)}, bf16[1024,128]{1,0:T(8,128)(2,1)}, u32[]{:S(2)}, u32[]{:S(2)}) collective-permute-start(bf16[1024,128]{1,0:T(8,128)(2,1)S(1)} %collective-permute-done.15), channel_id=1, source_target_pairs={{16,0},{32,16},{48,32},{0,48},{17,1},{33,17},{49,33},{1,49},{18,2}... | collective-permute-start | bytes 786440 | tf_op jit(solution)/shard_map/ppermute | solution.py:10
  39.0 19.8 %collective-permute-start.1 = (bf16[1024,128]{1,0:T(8,128)(2,1)S(1)}, bf16[1024,128]{1,0:T(8,128)(2,1)}, u32[]{:S(2)}, u32[]{:S(2)}) collective-permute-start(bf16[1024,128]{1,0:T(8,128)(2,1)S(1)} %collective-permute-done), channel_id=1, source_target_pairs={{48,0},{0,16},{16,32},{32,48},{49,1},{1,17},{17,33},{33,49},{50,2}... | collective-permute-start | bytes 786440 | tf_op jit(solution)/shard_map/ppermute | solution.py:10
  40.5 22.8 %collective-permute-start.4 = (bf16[1024,128]{1,0:T(8,128)(2,1)S(1)}, bf16[1024,128]{1,0:T(8,128)(2,1)}, u32[]{:S(2)}, u32[]{:S(2)}) collective-permute-start(bf16[1024,128]{1,0:T(8,128)(2,1)S(1)} %collective-permute-done.3), channel_id=1, source_target_pairs={{48,0},{0,16},{16,32},{32,48},{49,1},{1,17},{17,33},{33,49},{50,2}... | collective-permute-start | bytes 786440 | tf_op jit(solution)/shard_map/ppermute | solution.py:10
  45.0 28.3 %collective-permute-start.14 = (bf16[1024,128]{1,0:T(8,128)(2,1)}, bf16[1024,128]{1,0:T(8,128)(2,1)S(1)}, u32[]{:S(2)}, u32[]{:S(2)}) collective-permute-start(bf16[1024,128]{1,0:T(8,128)(2,1)} %collective-permute-done.13), channel_id=1, source_target_pairs={{12,0},{13,1},{14,2},{15,3},{0,4},{1,5},{2,6},{3,7},{4,8},{5,9},{6... | collective-permute-start | bytes 786440 | tf_op jit(solution)/shard_map/ppermute | solution.py:10
  55.9 20.1 %collective-permute-start.17 = (bf16[1024,128]{1,0:T(8,128)(2,1)}, bf16[1024,128]{1,0:T(8,128)(2,1)S(1)}, u32[]{:S(2)}, u32[]{:S(2)}) collective-permute-start(bf16[1024,128]{1,0:T(8,128)(2,1)} %collective-permute-done.16), channel_id=1, source_target_pairs={{4,0},{5,1},{6,2},{7,3},{8,4},{9,5},{10,6},{11,7},{12,8},{13,9},{1... | collective-permute-start | bytes 786440 | tf_op jit(solution)/shard_map/ppermute | solution.py:10
  58.8 20.1 %collective-permute-start.2 = (bf16[1024,128]{1,0:T(8,128)(2,1)}, bf16[1024,128]{1,0:T(8,128)(2,1)S(1)}, u32[]{:S(2)}, u32[]{:S(2)}) collective-permute-start(bf16[1024,128]{1,0:T(8,128)(2,1)} %collective-permute-done.1), channel_id=1, source_target_pairs={{15,0},{0,1},{1,2},{2,3},{3,4},{4,5},{5,6},{6,7},{7,8},{8,9},{9,10... | collective-permute-start | bytes 786440 | tf_op jit(solution)/shard_map/ppermute | solution.py:10
  63.3 18.7 %collective-permute-start.5 = (bf16[1024,128]{1,0:T(8,128)(2,1)}, bf16[1024,128]{1,0:T(8,128)(2,1)S(1)}, u32[]{:S(2)}, u32[]{:S(2)}) collective-permute-start(bf16[1024,128]{1,0:T(8,128)(2,1)} %collective-permute-done.4), channel_id=1, source_target_pairs={{7,0},{8,1},{9,2},{10,3},{11,4},{12,5},{13,6},{14,7},{15,8},{0,9},... | collective-permute-start | bytes 786440 | tf_op jit(solution)/shard_map/ppermute | solution.py:10
  113.9 17.0 %collective-permute-start.6 = (f32[64,128]{1,0:T(8,128)S(1)}, f32[64,128]{1,0:T(8,128)S(1)}, u32[]{:S(2)}, u32[]{:S(2)}) collective-permute-start(f32[64,128]{1,0:T(8,128)S(1)} %pad_maximum_fusion), channel_id=1, source_target_pairs={{64,0},{128,64},{192,128},{0,192},{65,1},{129,65},{193,129},{1,193... | collective-permute-start | bytes 98312 | tf_op jit(solution)/shard_map/ppermute | solution.py:10
  119.1 14.9 %collective-permute-start.9 = (f32[64,128]{1,0:T(8,128)S(1)}, f32[64,128]{1,0:T(8,128)S(1)}, u32[]{:S(2)}, u32[]{:S(2)}) collective-permute-start(f32[64,128]{1,0:T(8,128)S(1)} %pad_maximum_fusion.1), channel_id=1, source_target_pairs={{64,0},{128,64},{192,128},{0,192},{65,1},{129,65},{193,129},{1,193... | collective-permute-start | bytes 98312 | tf_op jit(solution)/shard_map/ppermute | solution.py:10
  123.9 10.3 %collective-permute-start.18 = (f32[64,128]{1,0:T(8,128)S(1)}, f32[64,128]{1,0:T(8,128)S(1)}, u32[]{:S(2)}, u32[]{:S(2)}) collective-permute-start(f32[64,128]{1,0:T(8,128)S(1)} %pad_maximum_fusion.2), channel_id=1, source_target_pairs={{128,0},{192,64},{0,128},{64,192},{129,1},{193,65},{1,129},{65,193... | collective-permute-start | bytes 98312 | tf_op jit(solution)/shard_map/ppermute | solution.py:10
  129.2 7.7 %collective-permute-start.21 = (f32[64,128]{1,0:T(8,128)S(1)}, f32[64,128]{1,0:T(8,128)S(1)}, u32[]{:S(2)}, u32[]{:S(2)}) collective-permute-start(f32[64,128]{1,0:T(8,128)S(1)} %pad_maximum_fusion.3), channel_id=1, source_target_pairs={{128,0},{192,64},{0,128},{64,192},{129,1},{193,65},{1,129},{65,193... | collective-permute-start | bytes 98312 | tf_op jit(solution)/shard_map/ppermute | solution.py:10
  130.9 8.4 %collective-permute-start.7 = (f32[64,128]{1,0:T(8,128)S(1)}, f32[64,128]{1,0:T(8,128)S(1)}, u32[]{:S(2)}, u32[]{:S(2)}) collective-permute-start(f32[64,128]{1,0:T(8,128)S(1)} %collective-permute-done.6), channel_id=1, source_target_pairs={{16,0},{32,16},{48,32},{0,48},{17,1},{33,17},{49,33},{1,49},{18,2}... | collective-permute-start | bytes 98312 | tf_op jit(solution)/shard_map/ppermute | solution.py:10
  134.0 5.4 %collective-permute-start.10 = (f32[64,128]{1,0:T(8,128)S(1)}, f32[64,128]{1,0:T(8,128)S(1)}, u32[]{:S(2)}, u32[]{:S(2)}) collective-permute-start(f32[64,128]{1,0:T(8,128)S(1)} %collective-permute-done.9), channel_id=1, source_target_pairs={{16,0},{32,16},{48,32},{0,48},{17,1},{33,17},{49,33},{1,49},{18,2}... | collective-permute-start | bytes 98312 | tf_op jit(solution)/shard_map/ppermute | solution.py:10
  134.2 6.0 %collective-permute-start.19 = (f32[64,128]{1,0:T(8,128)S(1)}, f32[64,128]{1,0:T(8,128)S(1)}, u32[]{:S(2)}, u32[]{:S(2)}) collective-permute-start(f32[64,128]{1,0:T(8,128)S(1)} %collective-permute-done.18), channel_id=1, source_target_pairs={{48,0},{0,16},{16,32},{32,48},{49,1},{1,17},{17,33},{33,49},{50,2}... | collective-permute-start | bytes 98312 | tf_op jit(solution)/shard_map/ppermute | solution.py:10
  136.9 6.3 %collective-permute-start.22 = (f32[64,128]{1,0:T(8,128)S(1)}, f32[64,128]{1,0:T(8,128)S(1)}, u32[]{:S(2)}, u32[]{:S(2)}) collective-permute-start(f32[64,128]{1,0:T(8,128)S(1)} %collective-permute-done.21), channel_id=1, source_target_pairs={{48,0},{0,16},{16,32},{32,48},{49,1},{1,17},{17,33},{33,49},{50,2}... | collective-permute-start | bytes 98312 | tf_op jit(solution)/shard_map/ppermute | solution.py:10
  139.3 5.7 %collective-permute-start.8 = (f32[64,128]{1,0:T(8,128)S(1)}, f32[64,128]{1,0:T(8,128)S(1)}, u32[]{:S(2)}, u32[]{:S(2)}) collective-permute-start(f32[64,128]{1,0:T(8,128)S(1)} %collective-permute-done.7), channel_id=1, source_target_pairs={{1,0},{2,1},{3,2},{4,3},{5,4},{6,5},{7,6},{8,7},{9,8},{10,9},{11,1... | collective-permute-start | bytes 98312 | tf_op jit(solution)/shard_map/ppermute | solution.py:10
  139.4 5.6 %collective-permute-start.11 = (f32[64,128]{1,0:T(8,128)S(1)}, f32[64,128]{1,0:T(8,128)S(1)}, u32[]{:S(2)}, u32[]{:S(2)}) collective-permute-start(f32[64,128]{1,0:T(8,128)S(1)} %collective-permute-done.10), channel_id=1, source_target_pairs={{9,0},{10,1},{11,2},{12,3},{13,4},{14,5},{15,6},{0,7},{1,8},{2,9},... | collective-permute-start | bytes 98312 | tf_op jit(solution)/shard_map/ppermute | solution.py:10
  140.2 5.6 %collective-permute-start.20 = (f32[64,128]{1,0:T(8,128)S(1)}, f32[64,128]{1,0:T(8,128)S(1)}, u32[]{:S(2)}, u32[]{:S(2)}) collective-permute-start(f32[64,128]{1,0:T(8,128)S(1)} %collective-permute-done.19), channel_id=1, source_target_pairs={{4,0},{5,1},{6,2},{7,3},{8,4},{9,5},{10,6},{11,7},{12,8},{13,9},{1... | collective-permute-start | bytes 98312 | tf_op jit(solution)/shard_map/ppermute | solution.py:10
  143.2 6.3 %collective-permute-start.23 = (f32[64,128]{1,0:T(8,128)S(1)}, f32[64,128]{1,0:T(8,128)S(1)}, u32[]{:S(2)}, u32[]{:S(2)}) collective-permute-start(f32[64,128]{1,0:T(8,128)S(1)} %collective-permute-done.22), channel_id=1, source_target_pairs={{12,0},{13,1},{14,2},{15,3},{0,4},{1,5},{2,6},{3,7},{4,8},{5,9},{6... | collective-permute-start | bytes 98312 | tf_op jit(solution)/shard_map/ppermute | solution.py:10
  (10 other events, 68.8 us)
where the time goes:
time: 151 us; the launch traced here: 150 us
  matrix products  49.4 us (33%)
  starting transfers between devices  36.4 us (24%)
  waiting for transfers between devices  25.8 us (17%)
  between operations  18.3 us (12%)
  local copies, waits for them, and re-layouts  14.3 us (9%)
  other arithmetic  6.39 us (4%)
    ppermute x24, starting transfers between devices, shifted(): return lax.ppermute(block, axis, route)  36.4 us
    ppermute x24, waiting for transfers between devices, shifted(): return lax.ppermute(block, axis, route)  25.8 us
    dot_general x4, matrix products, density_product(): jnp.dot(masked, swapped.T, preferred_element_type=jnp.float32)  24.2 us
    dot_general x4, matrix products, exchange_block(): lax.dot_general(orbital, mixture, (((0,), (0,)), ((), ())), preferred_ele...  14.3 us
    dot_general x4, matrix products, density_product(): jnp.dot(masked, orbital.T, preferred_element_type=jnp.float32)  10.8 us
    unnamed x22, local copies, waits for them, and re-layouts  6.82 us
    slice x1, local copies, waits for them, and re-layouts, on_device(): kernel_real = kernel[0, 0]  4.71 us
  transfers between devices with their start and end apart: 24, of which 7 were waited for; matrix products, arithmetic and copies ran while one was open for 23% of the time, Pallas kernels for 0%

commit v1 on v0

v1 whole, which is shorter than its diff:
```python
import functools

import jax
import jax.numpy as jnp
from jax import lax
from jax.experimental import pallas as pl
from jax.experimental.pallas import tpu as pltpu
from jax.sharding import PartitionSpec as P

MESH = pl.DeviceIdType.MESH
AXES = ("kx", "ky", "kz")
NT = (((1,), (1,)), ((), ()))
TN = (((0,), (0,)), ((), ()))
F32 = jnp.float32
BF16 = jnp.bfloat16
CHUNK = 256


def hop_shifts(turn, counts):
    forward = (
        (turn + 1) % counts[0],
        (2 * turn + 1) % counts[1],
        (3 * turn + 1) % counts[2],
    )
    partner = (forward[0], forward[1], (forward[2] - counts[2] // 2) % counts[2])
    return forward, partner


def exchange_kernel(counts, cells, shifts, orbitals, weights, plan, occupation, out, *scratch):
    (local, weight, occupied, sending, orbital, turned, masked, hadamard, first_sum, second_sum,
     block, returned, local_sem, weight_sem, occupied_sem, send_sem, recv_sem, back_send_sem, back_recv_sem) = scratch
    places = tuple(lax.axis_index(axis) for axis in AXES)
    points, nmu, width = orbitals.shape
    bands = width // 2
    chunks = nmu // CHUNK
    messages = len(shifts)
    turns = messages // 2

    def moved(shift, sign):
        return tuple(lax.rem(p + (sign * s) % n, n) for p, s, n in zip(places, shift, counts))

    def linear(place):
        return (place[0] * counts[1] + place[1]) * counts[2] + place[2]

    def slot_of(message, place):
        return plan[message // 2, message % 2, linear(place)]

    def rows(c):
        return pl.ds(pl.multiple_of(c * CHUNK, CHUNK), CHUNK)

    targets = [moved(shift, 1) for shift in shifts]
    sources = [moved(shift, -1) for shift in shifts]

    def orbital_copy(m, c):
        return pltpu.make_async_remote_copy(
            src_ref=sending.at[m, rows(c)],
            dst_ref=orbital.at[m, rows(c)],
            send_sem=send_sem.at[m, c],
            recv_sem=recv_sem.at[m, c],
            device_id=targets[m],
            device_id_type=MESH,
        )

    def block_copy(m):
        return pltpu.make_async_remote_copy(
            src_ref=block.at[m],
            dst_ref=returned.at[m],
            send_sem=back_send_sem.at[m],
            recv_sem=back_recv_sem.at[m],
            device_id=sources[m],
            device_id_type=MESH,
        )

    partners = {}
    for shift in shifts:
        for sign in (1, -1):
            partners[tuple((sign * s) % n for s, n in zip(shift, counts))] = moved(shift, sign)
    barrier = pltpu.get_barrier_semaphore()
    for partner in partners.values():
        pl.semaphore_signal(barrier, inc=1, device_id=partner, device_id_type=MESH)

    local_copy = pltpu.make_async_copy(orbitals, local, local_sem)
    local_copy.start()
    weight_copy = pltpu.make_async_copy(weights, weight, weight_sem)
    occupied_copies = []
    for m in range(messages):
        x, y, z = sources[m]
        occupied_copies.append(
            pltpu.make_async_copy(
                occupation.at[
                    pl.ds(x * cells[0], cells[0]),
                    pl.ds(y * cells[1], cells[1]),
                    pl.ds(pl.multiple_of(z // 8 * 8, 8), 8),
                ],
                occupied.at[m],
                occupied_sem.at[m],
            )
        )
    for copy in occupied_copies:
        copy.start()
    own_slots = [slot_of(m, places) for m in range(messages)]
    first_sum[...] = jnp.zeros_like(first_sum)
    second_sum[...] = jnp.zeros_like(second_sum)
    local_copy.wait()
    weight_copy.start()
    for m in range(0, messages, 2):
        sending[m] = local[own_slots[m]]
    pl.semaphore_wait(barrier, len(partners))
    for c in range(chunks):
        for m in range(0, messages, 2):
            orbital_copy(m, c).start()
    for m in range(1, messages, 2):
        sending[m] = local[own_slots[m]]
    for c in range(chunks):
        for m in range(1, messages, 2):
            orbital_copy(m, c).start()

    masks = []
    for copy in occupied_copies:
        copy.wait()
    for m in range(messages):
        slot = slot_of(m, sources[m])
        row = occupied[
            m, lax.div(slot, cells[1]), lax.rem(slot, cells[1]), pl.ds(lax.rem(sources[m][2], 8), 1)
        ].astype(F32)
        masks.append(jnp.concatenate([row, row], axis=1).astype(BF16))
    weight_copy.wait()

    def prepare(m, c):
        orbital_copy(m, c).wait_recv()
        part = orbital[m, rows(c)]
        turned[m, rows(c)] = jnp.concatenate([-part[:, bands:], part[:, :bands]], axis=1)
        masked[m, rows(c)] = part * masks[m]

    def stacked(m, j):
        return jnp.concatenate([orbital[m, rows(j)], turned[m, rows(j)]], axis=0)

    def product(m, i, j, sign):
        density = lax.dot_general(
            masked[m, rows(i)], stacked(m, j), NT, preferred_element_type=F32
        )
        real, imag = density[:, :CHUNK], density[:, CHUNK:]
        wr = weight[0, rows(i), rows(j)].astype(F32)
        wi = weight[1, rows(i), rows(j)].astype(F32) * sign
        return jnp.concatenate(
            [(wr * real - wi * imag).astype(BF16), (wr * imag + wi * real).astype(BF16)], axis=1
        )

    def first_step(turn, i, j):
        hadamard[turn, j, rows(i)] = product(2 * turn, i, j, -1.0)

    def second_step(turn, i, j):
        first_sum[turn, rows(i)] += jnp.dot(
            product(2 * turn + 1, i, j, 1.0), stacked(2 * turn, j), preferred_element_type=F32
        )

    def panels(step, turn, c):
        @pl.loop(0, c)
        def _(i):
            step(turn, i, c)

        @pl.loop(0, c + 1)
        def _(j):
            step(turn, c, j)

    @pl.loop(0, chunks)
    def _(c):
        for turn in range(turns):
            prepare(2 * turn, c)
            panels(first_step, turn, c)

    @pl.loop(0, chunks)
    def _(c):
        for turn in range(turns):
            prepare(2 * turn + 1, c)
            second_sum[turn] += jnp.dot(
                hadamard[turn, c], stacked(2 * turn + 1, c), preferred_element_type=F32
            )
            panels(second_step, turn, c)

    for turn in range(turns):
        for m, total in ((2 * turn, first_sum), (2 * turn + 1, second_sum)):
            gram = lax.dot_general(
                orbital[m], total[turn].astype(BF16), TN, preferred_element_type=F32
            )
            real = -(gram[:bands, :bands] + gram[bands:, bands:])
            imag = -(gram[:bands, bands:] - gram[bands:, :bands])
            block[m] = jnp.concatenate([real, imag], axis=1)
            block_copy(m).start()

    for m in range(messages):
        block_copy(m).wait_recv()
    for s in range(points):
        total = jnp.zeros((bands, width), F32)
        for m in range(messages):
            total = total + jnp.where(own_slots[m] == s, returned[m], 0.0)
        out[s] = total
    for m in range(messages):
        for c in range(chunks):
            orbital_copy(m, c).wait_send()
        block_copy(m).wait_send()


def on_device(counts, orbitals, kernel, plan, occupation):
    cells = orbitals.shape[:3]
    points = cells[0] * cells[1] * cells[2]
    nmu, width = orbitals.shape[3:]
    turns = plan.shape[0]
    shifts = [shift for turn in range(turns) for shift in hop_shifts(turn, counts)]
    messages = len(shifts)
    chunks = nmu // CHUNK
    result = pl.pallas_call(
        functools.partial(exchange_kernel, counts, cells, shifts),
        out_shape=jax.ShapeDtypeStruct((points, width // 2, width), F32),
        in_specs=[
            pl.BlockSpec(memory_space=pl.ANY),
            pl.BlockSpec(memory_space=pl.ANY),
            pl.BlockSpec(memory_space=pltpu.SMEM),
            pl.BlockSpec(memory_space=pl.ANY),
        ],
        out_specs=pl.BlockSpec(memory_space=pltpu.VMEM),
        scratch_shapes=[
            pltpu.VMEM((points, nmu, width), BF16),
            pltpu.VMEM((2, nmu, nmu), BF16),
            pltpu.VMEM((messages, cells[0], cells[1], 8, width // 2), jnp.int32),
            pltpu.VMEM((messages, nmu, width), BF16),
            pltpu.VMEM((messages, nmu, width), BF16),
            pltpu.VMEM((messages, nmu, width), BF16),
            pltpu.VMEM((messages, nmu, width), BF16),
            pltpu.VMEM((turns, chunks, nmu, 2 * CHUNK), BF16),
            pltpu.VMEM((turns, nmu, width), F32),
            pltpu.VMEM((turns, nmu, width), F32),
            pltpu.VMEM((messages, width // 2, width), F32),
            pltpu.VMEM((messages, width // 2, width), F32),
            pltpu.SemaphoreType.DMA,
            pltpu.SemaphoreType.DMA,
            pltpu.SemaphoreType.DMA((messages,)),
            pltpu.SemaphoreType.DMA((messages, chunks)),
            pltpu.SemaphoreType.DMA((messages, chunks)),
            pltpu.SemaphoreType.DMA((messages,)),
            pltpu.SemaphoreType.DMA((messages,)),
        ],
        compiler_params=pltpu.CompilerParams(
            collective_id=0, has_side_effects=True, vmem_limit_bytes=56 * 2**20
        ),
        name="exchange",
    )(orbitals.reshape(points, nmu, width), kernel[0], plan, occupation)
    return result.reshape(*cells, width // 2, width)


def solution(mesh):
    counts = tuple(mesh.shape[axis] for axis in AXES)
    return jax.shard_map(
        functools.partial(on_device, counts),
        mesh=mesh,
        in_specs=(P(*AXES, None, None), P(AXES, None, None, None), P(), P()),
        out_specs=P(*AXES, None, None),
        check_vma=False,
    )
```

time: 151 us -> 64.7 us (0.43)
  the two profiles are of different devices: /device:TPU:32 before, /device:TPU:17 now
where the time goes in v1:
time: 64.7 us; the launch traced here: 64.5 us
  Pallas kernels  62.6 us (97%)
  local copies, waits for them, and re-layouts  1.89 us (3%)
    pallas_call x1, Pallas kernels, on_device(): pl.pallas_call(functools.partial(exchange_kernel, counts, cells, shifts),...  62.6 us
    unnamed x1, local copies, waits for them, and re-layouts  1.89 us

profile of v1, /device:TPU:17, one launch (start us, length us, event | category | flops | bytes accessed | tf_op | source)
XLA Modules:
  0.0 64.5 jit_solution(6781579071400356662)
XLA Ops:
  0.0 62.6 %exchange.1 = f32[16,64,128]{2,1,0:T(8,128)} custom-call(bf16[16,1024,128]{2,1,0:T(8,128)(2,1)} %bitcast.5, bf16[2,1024,1024]{2,1,0:T(8,128)(2,1)} %bitcast.6, s32[2,2,256]{2,1,0:T(2,128)} %plan.1, s32[16,16,16,64]{3,2,1,0:T(8,128)} %occupation.1), custom_call_target="tpu_custom_call" | custom-call | tf_op jit(solution)/shard_map/exchange/pallas_call | solution.py:212
  62.6 1.9 %copy.7 = f32[4,4,1,64,128]{4,3,2,1,0:T(8,128)} copy(f32[4,4,1,64,128]{4,3,2,1,0:T(8,128)} %bitcast.7) | data formatting | bytes 1048576

commit v2 on v1

--- a/solution.py
+++ b/solution.py
@@ -27,7 +27,7 @@
 
 
 def exchange_kernel(counts, cells, shifts, orbitals, weights, plan, occupation, out, *scratch):
-    (local, weight, occupied, sending, orbital, turned, masked, hadamard, first_sum, second_sum,
+    (local, weight, occupied, mask_rows, sending, orbital, turned, masked, hadamard, first_sum, second_sum,
      block, returned, local_sem, weight_sem, occupied_sem, send_sem, recv_sem, back_send_sem, back_recv_sem) = scratch
     places = tuple(lax.axis_index(axis) for axis in AXES)
     points, nmu, width = orbitals.shape
@@ -46,18 +46,19 @@
         return plan[message // 2, message % 2, linear(place)]
 
     def rows(c):
-        return pl.ds(pl.multiple_of(c * CHUNK, CHUNK), CHUNK)
+        return pl.ds(c * CHUNK, CHUNK)
 
     targets = [moved(shift, 1) for shift in shifts]
     sources = [moved(shift, -1) for shift in shifts]
 
     def orbital_copy(m, c):
+        target = targets[m] if isinstance(m, int) else targets[0]
         return pltpu.make_async_remote_copy(
             src_ref=sending.at[m, rows(c)],
             dst_ref=orbital.at[m, rows(c)],
             send_sem=send_sem.at[m, c],
             recv_sem=recv_sem.at[m, c],
-            device_id=targets[m],
+            device_id=target,
             device_id_type=MESH,
         )
 
@@ -99,8 +100,6 @@
     for copy in occupied_copies:
         copy.start()
     own_slots = [slot_of(m, places) for m in range(messages)]
-    first_sum[...] = jnp.zeros_like(first_sum)
-    second_sum[...] = jnp.zeros_like(second_sum)
     local_copy.wait()
     weight_copy.start()
     for m in range(0, messages, 2):
@@ -115,7 +114,6 @@
         for m in range(1, messages, 2):
             orbital_copy(m, c).start()
 
-    masks = []
     for copy in occupied_copies:
         copy.wait()
     for m in range(messages):
@@ -123,60 +121,66 @@
         row = occupied[
             m, lax.div(slot, cells[1]), lax.rem(slot, cells[1]), pl.ds(lax.rem(sources[m][2], 8), 1)
         ].astype(F32)
-        masks.append(jnp.concatenate([row, row], axis=1).astype(BF16))
+        mask_rows[m] = jnp.concatenate([row, row], axis=1)
     weight_copy.wait()
 
     def prepare(m, c):
         orbital_copy(m, c).wait_recv()
         part = orbital[m, rows(c)]
         turned[m, rows(c)] = jnp.concatenate([-part[:, bands:], part[:, :bands]], axis=1)
-        masked[m, rows(c)] = part * masks[m]
-
-    def stacked(m, j):
-        return jnp.concatenate([orbital[m, rows(j)], turned[m, rows(j)]], axis=0)
-
-    def product(m, i, j, sign):
+        masked[m, rows(c)] = part * mask_rows[m].astype(BF16)
+
+    def stacked(m, low, high):
+        return jnp.concatenate([orbital[m, low:high], turned[m, low:high]], axis=0)
+
+    def product(m, top, bottom, low, high, sign):
         density = lax.dot_general(
-            masked[m, rows(i)], stacked(m, j), NT, preferred_element_type=F32
-        )
-        real, imag = density[:, :CHUNK], density[:, CHUNK:]
-        wr = weight[0, rows(i), rows(j)].astype(F32)
-        wi = weight[1, rows(i), rows(j)].astype(F32) * sign
-        return jnp.concatenate(
-            [(wr * real - wi * imag).astype(BF16), (wr * imag + wi * real).astype(BF16)], axis=1
-        )
-
-    def first_step(turn, i, j):
-        hadamard[turn, j, rows(i)] = product(2 * turn, i, j, -1.0)
-
-    def second_step(turn, i, j):
-        first_sum[turn, rows(i)] += jnp.dot(
-            product(2 * turn + 1, i, j, 1.0), stacked(2 * turn, j), preferred_element_type=F32
-        )
-
-    def panels(step, turn, c):
-        @pl.loop(0, c)
-        def _(i):
-            step(turn, i, c)
-
-        @pl.loop(0, c + 1)
-        def _(j):
-            step(turn, c, j)
-
-    @pl.loop(0, chunks)
-    def _(c):
-        for turn in range(turns):
-            prepare(2 * turn, c)
-            panels(first_step, turn, c)
-
-    @pl.loop(0, chunks)
-    def _(c):
-        for turn in range(turns):
-            prepare(2 * turn + 1, c)
-            second_sum[turn] += jnp.dot(
-                hadamard[turn, c], stacked(2 * turn + 1, c), preferred_element_type=F32
+            masked[m, top:bottom], stacked(m, low, high), NT, preferred_element_type=F32
+        )
+        span = high - low
+        real, imag = density[:, :span], density[:, span:]
+        wr = weight[0, top:bottom, low:high].astype(F32)
+        wi = weight[1, top:bottom, low:high].astype(F32) * sign
+        return (wr * real - wi * imag).astype(BF16), (wr * imag + wi * real).astype(BF16)
+
+    for c in range(chunks):
+        low, high = c * CHUNK, (c + 1) * CHUNK
+
+        @pl.loop(0, turns)
+        def _(turn):
+            m = 2 * turn
+            prepare(m, c)
+            real, imag = product(m, 0, high, low, high, -1.0)
+            hadamard[turn, c, :high, :CHUNK] = real
+            hadamard[turn, c, :high, CHUNK:] = imag
+            if c:
+                real, imag = product(m, low, high, 0, low, -1.0)
+                for j in range(c):
+                    part = slice(j * CHUNK, (j + 1) * CHUNK)
+                    hadamard[turn, j, low:high, :CHUNK] = real[:, part]
+                    hadamard[turn, j, low:high, CHUNK:] = imag[:, part]
+
+    for c in range(chunks):
+        low, high = c * CHUNK, (c + 1) * CHUNK
+
+        @pl.loop(0, turns)
+        def _(turn):
+            k, m = 2 * turn, 2 * turn + 1
+            prepare(m, c)
+            mixed = jnp.dot(hadamard[turn, c], stacked(m, low, high), preferred_element_type=F32)
+            second_sum[turn] = mixed if c == 0 else second_sum[turn] + mixed
+            real, imag = product(m, 0, high, low, high, 1.0)
+            mixed = jnp.dot(
+                jnp.concatenate([real, imag], axis=1), stacked(k, low, high), preferred_element_type=F32
             )
-            panels(second_step, turn, c)
+            if c:
+                first_sum[turn, :low] += mixed[:low]
+                real, imag = product(m, low, high, 0, low, 1.0)
+                first_sum[turn, low:high] = mixed[low:] + jnp.dot(
+                    jnp.concatenate([real, imag], axis=1), stacked(k, 0, low), preferred_element_type=F32
+                )
+            else:
+                first_sum[turn, :high] = mixed
 
     for turn in range(turns):
         for m, total in ((2 * turn, first_sum), (2 * turn + 1, second_sum)):
@@ -223,6 +227,7 @@
             pltpu.VMEM((points, nmu, width), BF16),
             pltpu.VMEM((2, nmu, nmu), BF16),
             pltpu.VMEM((messages, cells[0], cells[1], 8, width // 2), jnp.int32),
+            pltpu.VMEM((messages, 1, width), F32),
             pltpu.VMEM((messages, nmu, width), BF16),
             pltpu.VMEM((messages, nmu, width), BF16),
             pltpu.VMEM((messages, nmu, width), BF16),

time: 64.7 us -> 57.9 us (0.89)
  the two profiles are of different devices: /device:TPU:17 before, /device:TPU:32 now
where the time goes in v2:
time: 57.9 us; the launch traced here: 56.8 us
  Pallas kernels  54.9 us (95%)
  local copies, waits for them, and re-layouts  1.89 us (3%)
    pallas_call x1, Pallas kernels, on_device(): pl.pallas_call(functools.partial(exchange_kernel, counts, cells, shifts),...  54.9 us
    unnamed x1, local copies, waits for them, and re-layouts  1.89 us

profile of v2, /device:TPU:32, one launch (start us, length us, event | category | flops | bytes accessed | tf_op | source)
XLA Modules:
  0.0 56.8 jit_solution(11275598203532583151)
XLA Ops:
  0.0 54.9 %exchange.1 = f32[16,64,128]{2,1,0:T(8,128)} custom-call(bf16[16,1024,128]{2,1,0:T(8,128)(2,1)} %bitcast.5, bf16[2,1024,1024]{2,1,0:T(8,128)(2,1)} %bitcast.6, s32[2,2,256]{2,1,0:T(2,128)} %plan.1, s32[16,16,16,64]{3,2,1,0:T(8,128)} %occupation.1), custom_call_target="tpu_custom_call" | custom-call | tf_op jit(solution)/shard_map/exchange/pallas_call | solution.py:216
  54.9 1.9 %copy.7 = f32[4,4,1,64,128]{4,3,2,1,0:T(8,128)} copy(f32[4,4,1,64,128]{4,3,2,1,0:T(8,128)} %bitcast.7) | data formatting | bytes 1048576

commit v3 on v2

v3 whole, which is shorter than its diff:
```python
import functools

import jax
import jax.numpy as jnp
from jax import lax
from jax.experimental import pallas as pl
from jax.experimental.pallas import tpu as pltpu
from jax.sharding import PartitionSpec as P

MESH = pl.DeviceIdType.MESH
AXES = ("kx", "ky", "kz")
NT = (((1,), (1,)), ((), ()))
F32 = jnp.float32
BF16 = jnp.bfloat16
PIECE = 128
UNITS = (256, 256, 256, 128, 128)
ORDER = (0, 3, 2, 1)


def hop_shifts(turn, counts):
    forward = (
        (turn + 1) % counts[0],
        (2 * turn + 1) % counts[1],
        (3 * turn + 1) % counts[2],
    )
    partner = (forward[0], forward[1], (forward[2] - counts[2] // 2) % counts[2])
    return forward, partner


def exchange_kernel(counts, cells, shifts, orbitals, weights, plan, occupation, out, slots, *scratch):
    pieces = orbitals.shape[1] // PIECE
    local, scratch = scratch[:pieces], scratch[pieces:]
    (weight, weight_flipped, occupied, mask_rows, sending, orbital, turned, masked, flipped, flipped_turned, sums, block,
     returned, local_sem, weight_sem, occupied_sem, send_sem, recv_sem, back_send_sem, back_recv_sem) = scratch
    places = tuple(lax.axis_index(axis) for axis in AXES)
    points, nmu, width = orbitals.shape
    bands = width // 2
    messages = len(shifts)
    turns = messages // 2

    def moved(shift, sign):
        return tuple(lax.rem(p + (sign * s) % n, n) for p, s, n in zip(places, shift, counts))

    def linear(place):
        return (place[0] * counts[1] + place[1]) * counts[2] + place[2]

    def slot_of(message, place):
        return plan[message // 2, message % 2, linear(place)]

    def rows(c):
        return pl.ds(c * PIECE, PIECE)

    targets = [moved(shift, 1) for shift in shifts]
    sources = [moved(shift, -1) for shift in shifts]

    def orbital_copy(m, c):
        target = targets[m] if isinstance(m, int) else targets[0]
        return pltpu.make_async_remote_copy(
            src_ref=sending.at[m, rows(c)],
            dst_ref=orbital.at[m, rows(c)],
            send_sem=send_sem.at[m, c],
            recv_sem=recv_sem.at[m, c],
            device_id=target,
            device_id_type=MESH,
        )

    def block_copy(m):
        return pltpu.make_async_remote_copy(
            src_ref=block.at[m],
            dst_ref=returned.at[m],
            send_sem=back_send_sem.at[m],
            recv_sem=back_recv_sem.at[m],
            device_id=sources[m],
            device_id_type=MESH,
        )

    partners = {}
    for shift in shifts:
        for sign in (1, -1):
            partners[tuple((sign * s) % n for s, n in zip(shift, counts))] = moved(shift, sign)
    barrier = pltpu.get_barrier_semaphore()
    for partner in partners.values():
        pl.semaphore_signal(barrier, inc=1, device_id=partner, device_id_type=MESH)

    local_copies = [
        pltpu.make_async_copy(orbitals.at[:, rows(c)], local[c], local_sem.at[c])
        for c in range(pieces)
    ]
    for copy in local_copies:
        copy.start()
    weight_copy = pltpu.make_async_copy(weights, weight, weight_sem)
    occupied_copies = []
    for m in range(messages):
        x, y, z = sources[m]
        occupied_copies.append(
            pltpu.make_async_copy(
                occupation.at[
                    pl.ds(x * cells[0], cells[0]),
                    pl.ds(y * cells[1], cells[1]),
                    pl.ds(pl.multiple_of(z // 8 * 8, 8), 8),
                ],
                occupied.at[m],
                occupied_sem.at[m],
            )
        )
    for copy in occupied_copies:
        copy.start()
    own_slots = [slot_of(m, places) for m in range(messages)]
    for c in range(pieces):
        local_copies[c].wait()
        for m in range(messages):
            sending[m, rows(c)] = local[c][own_slots[m]]
        if c == 0:
            pl.semaphore_wait(barrier, len(partners))
        for m in ORDER:
            orbital_copy(m, c).start()
    weight_copy.start()

    for m in range(messages):
        numbers = lax.broadcasted_iota(jnp.int32, slots.shape[1:], 0)
        slots[m] = jnp.where(numbers == own_slots[m], 1.0, 0.0)
    for copy in occupied_copies:
        copy.wait()
    for m in range(messages):
        slot = slot_of(m, sources[m])
        row = occupied[
            m, lax.div(slot, cells[1]), lax.rem(slot, cells[1]), pl.ds(lax.rem(sources[m][2], 8), 1)
        ].astype(F32)
        mask_rows[m] = jnp.concatenate([row, row], axis=1)
    weight_copy.wait()
    low = UNITS[0]
    for size in UNITS[1:]:
        for part in range(2):
            weight_flipped[part, :low, low : low + size] = weight[part, low : low + size, :low].T
        low += size

    def prepare(m, low, high):
        for c in range(low // PIECE, high // PIECE):
            orbital_copy(m, c).wait_recv()
        part = orbital[m, low:high]
        turned[m, low:high] = jnp.concatenate([-part[:, bands:], part[:, :bands]], axis=1)
        masked[m, low:high] = part * mask_rows[m].astype(BF16)
        part = part.T
        flipped[m, :, low:high] = part
        flipped_turned[m, :, low:high] = jnp.concatenate([-part[bands:], part[:bands]], axis=0)

    def stacked(m, low, high):
        return jnp.concatenate([orbital[m, low:high], turned[m, low:high]], axis=0)

    def extend(m, other, sign, low, high):
        size = high - low
        density = lax.dot_general(
            masked[m, :high], stacked(m, low, high), NT, preferred_element_type=F32
        )
        real, imag = density[:, :size], density[:, size:]
        wr = weight[0, :high, low:high].astype(F32)
        wi = weight[1, :high, low:high].astype(F32) * sign
        hadamard = jnp.concatenate(
            [(wr * real - wi * imag).astype(BF16), (wr * imag + wi * real).astype(BF16)], axis=1
        )
        column = jnp.dot(hadamard, stacked(other, low, high), preferred_element_type=F32)
        if low == 0:
            sums[other, :high] = column
            return
        sums[other, :low] += column[:low]
        real, imag = real[:low], imag[:low]
        wr = weight_flipped[0, :low, low:high].astype(F32)
        wi = weight_flipped[1, :low, low:high].astype(F32) * sign
        hadamard = jnp.concatenate(
            [(wr * real + wi * imag).astype(BF16), (wi * real - wr * imag).astype(BF16)], axis=0
        )
        before = jnp.concatenate([flipped[other, :, :low], flipped_turned[other, :, :low]], axis=1)
        row = jnp.dot(before, hadamard, preferred_element_type=F32)
        sums[other, low:high] = column[low:] + row.T

    def unit(turn, low, high):
        k, p = 2 * turn, 2 * turn + 1
        prepare(k, low, high)
        prepare(p, low, high)
        extend(p, k, 1.0, low, high)
        extend(k, p, -1.0, low, high)

    low = 0
    for size in UNITS[:-1]:
        high = low + size

        @pl.loop(0, turns)
        def _(turn):
            unit(turn, low, high)

        low = high

    for turn in reversed(range(turns)):
        unit(turn, low, nmu)
        for m in (2 * turn, 2 * turn + 1):
            gram = jnp.dot(flipped[m], sums[m].astype(BF16), preferred_element_type=F32)
            real = -(gram[:bands, :bands] + gram[bands:, bands:])
            imag = -(gram[:bands, bands:] - gram[bands:, :bands])
            block[m] = jnp.concatenate([real, imag], axis=1).astype(BF16)
            block_copy(m).start()

    for m in range(messages):
        block_copy(m).wait_recv()
        out[m] = returned[m].astype(F32)
    for m in range(messages):
        for c in range(pieces):
            orbital_copy(m, c).wait_send()
        block_copy(m).wait_send()


def on_device(counts, orbitals, kernel, plan, occupation):
    cells = orbitals.shape[:3]
    points = cells[0] * cells[1] * cells[2]
    nmu, width = orbitals.shape[3:]
    turns = plan.shape[0]
    shifts = [shift for turn in range(turns) for shift in hop_shifts(turn, counts)]
    messages = len(shifts)
    pieces = nmu // PIECE
    blocks, slots = pl.pallas_call(
        functools.partial(exchange_kernel, counts, cells, shifts),
        out_shape=(
            jax.ShapeDtypeStruct((messages, width // 2, width), F32),
            jax.ShapeDtypeStruct((messages, points, width), F32),
        ),
        in_specs=[
            pl.BlockSpec(memory_space=pl.ANY),
            pl.BlockSpec(memory_space=pl.ANY),
            pl.BlockSpec(memory_space=pltpu.SMEM),
            pl.BlockSpec(memory_space=pl.ANY),
        ],
        out_specs=(pl.BlockSpec(memory_space=pltpu.VMEM),) * 2,
        scratch_shapes=[pltpu.VMEM((points, PIECE, width), BF16)] * pieces
        + [
            pltpu.VMEM((2, nmu, nmu), BF16),
            pltpu.VMEM((2, nmu, nmu), BF16),
            pltpu.VMEM((messages, cells[0], cells[1], 8, width // 2), jnp.int32),
            pltpu.VMEM((messages, 1, width), F32),
            pltpu.VMEM((messages, nmu, width), BF16),
            pltpu.VMEM((messages, nmu, width), BF16),
            pltpu.VMEM((messages, nmu, width), BF16),
            pltpu.VMEM((messages, nmu, width), BF16),
            pltpu.VMEM((messages, width, nmu), BF16),
            pltpu.VMEM((messages, width, nmu), BF16),
            pltpu.VMEM((messages, nmu, width), F32),
            pltpu.VMEM((messages, width // 2, width), BF16),
            pltpu.VMEM((messages, width // 2, width), BF16),
            pltpu.SemaphoreType.DMA((pieces,)),
            pltpu.SemaphoreType.DMA,
            pltpu.SemaphoreType.DMA((messages,)),
            pltpu.SemaphoreType.DMA((messages, pieces)),
            pltpu.SemaphoreType.DMA((messages, pieces)),
            pltpu.SemaphoreType.DMA((messages,)),
            pltpu.SemaphoreType.DMA((messages,)),
        ],
        compiler_params=pltpu.CompilerParams(
            collective_id=0, has_side_effects=True, vmem_limit_bytes=56 * 2**20
        ),
        name="exchange",
    )(orbitals.reshape(points, nmu, width), kernel[0], plan, occupation)
    total = jnp.sum(slots[:, :, None, :] * blocks[:, None], axis=0)
    return total.reshape(*cells, width // 2, width)


def solution(mesh):
    counts = tuple(mesh.shape[axis] for axis in AXES)
    return jax.shard_map(
        functools.partial(on_device, counts),
        mesh=mesh,
        in_specs=(P(*AXES, None, None), P(AXES, None, None, None), P(), P()),
        out_specs=P(*AXES, None, None),
        check_vma=False,
    )
```

time: 57.9 us -> 52.2 us (0.902)
  Pallas kernels: 54.9 us -> 49.6 us
  other arithmetic: 0 us -> 1.91 us
  local copies, waits for them, and re-layouts: 1.89 us -> 0 us
    pallas_call x1, Pallas kernels: 54.9 us -> 49.6 us  [on_device(): pl.pallas_call(functools.partial(exchange_kernel, counts, cells, shifts),...]
    reduce_sum x0 -> x1, other arithmetic: none -> 1.91 us  [on_device(): total = jnp.sum(slots[:, :, None, :] * blocks[:, None], axis=0)]
    unnamed x1 -> x0, local copies, waits for them, and re-layouts: 1.89 us -> none
where the time goes in v3:
time: 52.2 us; the launch traced here: 51.6 us
  Pallas kernels  49.6 us (95%)
  other arithmetic  1.91 us (4%)
    pallas_call x1, Pallas kernels, on_device(): pl.pallas_call(functools.partial(exchange_kernel, counts, cells, shifts),...  49.6 us
    reduce_sum x1, other arithmetic, on_device(): total = jnp.sum(slots[:, :, None, :] * blocks[:, None], axis=0)  1.91 us

profile of v3, /device:TPU:32, one launch (start us, length us, event | category | flops | bytes accessed | tf_op | source)
XLA Modules:
  0.0 51.6 jit_solution(12676168943761219497)
XLA Ops:
  0.0 49.6 %exchange.1 = (f32[4,64,128]{2,1,0:T(8,128)}, f32[4,16,128]{2,1,0:T(8,128)}) custom-call(bf16[16,1024,128]{2,1,0:T(8,128)(2,1)} %bitcast.5, bf16[2,1024,1024]{2,1,0:T(8,128)(2,1)} %bitcast.6, s32[2,2,256]{2,1,0:T(2,128)} %plan.1, s32[16,16,16,64]{3,2,1,0:T(8,128)} %occupation.1), custom_call_target="tpu_custom_call" | custom-call | tf_op jit(solution)/shard_map/exchange/pallas_call | solution.py:219
  49.6 1.9 %multiply_reduce_fusion = f32[16,64,128]{2,1,0:T(8,128)} fusion(f32[4,64,128]{2,1,0:T(8,128)} %get-tuple-element.8, f32[4,16,128]{2,1,0:T(8,128)} %get-tuple-element.7), kind=kLoop, calls=%fused_computation | loop fusion | flops 917504 | bytes 688128 | tf_op jit(solution)/shard_map/reduce_sum | solution.py:260

commit v4 on v3

--- a/solution.py
+++ b/solution.py
@@ -13,7 +13,7 @@
 F32 = jnp.float32
 BF16 = jnp.bfloat16
 PIECE = 128
-UNITS = (256, 256, 256, 128, 128)
+UNITS = (256, 256, 128, 128, 128, 128)
 ORDER = (0, 3, 2, 1)
 
 
@@ -27,11 +27,11 @@
     return forward, partner
 
 
-def exchange_kernel(counts, cells, shifts, orbitals, weights, plan, occupation, out, slots, *scratch):
+def exchange_kernel(counts, cells, shifts, orbitals, weights, plan_table, occupation, out, slots, *scratch):
     pieces = orbitals.shape[1] // PIECE
     local, scratch = scratch[:pieces], scratch[pieces:]
-    (weight, weight_flipped, occupied, mask_rows, sending, orbital, turned, masked, flipped, flipped_turned, sums, block,
-     returned, local_sem, weight_sem, occupied_sem, send_sem, recv_sem, back_send_sem, back_recv_sem) = scratch
+    (plan, weight, weight_flipped, occupied, mask_rows, sending, orbital, turned, masked, flipped, flipped_turned, sums, block,
+     returned, plan_sem, local_sem, weight_sem, occupied_sem, send_sem, recv_sem, back_send_sem, back_recv_sem) = scratch
     places = tuple(lax.axis_index(axis) for axis in AXES)
     points, nmu, width = orbitals.shape
     bands = width // 2
@@ -82,6 +82,8 @@
     for partner in partners.values():
         pl.semaphore_signal(barrier, inc=1, device_id=partner, device_id_type=MESH)
 
+    plan_copy = pltpu.make_async_copy(plan_table, plan, plan_sem)
+    plan_copy.start()
     local_copies = [
         pltpu.make_async_copy(orbitals.at[:, rows(c)], local[c], local_sem.at[c])
         for c in range(pieces)
@@ -105,6 +107,7 @@
         )
     for copy in occupied_copies:
         copy.start()
+    plan_copy.wait()
     own_slots = [slot_of(m, places) for m in range(messages)]
     for c in range(pieces):
         local_copies[c].wait()
@@ -225,12 +228,13 @@
         in_specs=[
             pl.BlockSpec(memory_space=pl.ANY),
             pl.BlockSpec(memory_space=pl.ANY),
-            pl.BlockSpec(memory_space=pltpu.SMEM),
+            pl.BlockSpec(memory_space=pl.ANY),
             pl.BlockSpec(memory_space=pl.ANY),
         ],
         out_specs=(pl.BlockSpec(memory_space=pltpu.VMEM),) * 2,
         scratch_shapes=[pltpu.VMEM((points, PIECE, width), BF16)] * pieces
         + [
+            pltpu.SMEM(plan.shape, jnp.int32),
             pltpu.VMEM((2, nmu, nmu), BF16),
             pltpu.VMEM((2, nmu, nmu), BF16),
             pltpu.VMEM((messages, cells[0], cells[1], 8, width // 2), jnp.int32),
@@ -244,6 +248,7 @@
             pltpu.VMEM((messages, nmu, width), F32),
             pltpu.VMEM((messages, width // 2, width), BF16),
             pltpu.VMEM((messages, width // 2, width), BF16),
+            pltpu.SemaphoreType.DMA,
             pltpu.SemaphoreType.DMA((pieces,)),
             pltpu.SemaphoreType.DMA,
             pltpu.SemaphoreType.DMA((messages,)),
@@ -253,7 +258,7 @@
             pltpu.SemaphoreType.DMA((messages,)),
         ],
         compiler_params=pltpu.CompilerParams(
-            collective_id=0, has_side_effects=True, vmem_limit_bytes=56 * 2**20
+            collective_id=0, has_side_effects=True, vmem_limit_bytes=54000 * 2**10
         ),
         name="exchange",
     )(orbitals.reshape(points, nmu, width), kernel[0], plan, occupation)

time: 52.2 us -> 49.4 us (0.946); the launches traced: 51.6 us -> 49.3 us
  Pallas kernels: 49.6 us -> 47.7 us
  other arithmetic: 1.91 us -> 0.95 us
  local copies, waits for them, and re-layouts: 0 us -> 0.69 us
    pallas_call x1, Pallas kernels: 49.6 us -> 47.7 us  [on_device(): pl.pallas_call(functools.partial(exchange_kernel, counts, cells, shifts),...]
    reduce_sum x1, other arithmetic: 1.91 us -> 0.95 us  [on_device(): total = jnp.sum(slots[:, :, None, :] * blocks[:, None], axis=0)]
    unnamed x0 -> x2, local copies, waits for them, and re-layouts: none -> 0.69 us
where the time goes in v4:
time: 49.4 us; the launch traced here: 49.3 us
  Pallas kernels  47.7 us (97%)
  other arithmetic  0.95 us (2%)
  local copies, waits for them, and re-layouts  0.69 us (1%)
    pallas_call x1, Pallas kernels, on_device(): pl.pallas_call(functools.partial(exchange_kernel, counts, cells, shifts),...  47.7 us

profile of v4, /device:TPU:32, one launch (start us, length us, event | category | flops | bytes accessed | tf_op | source)
XLA Modules:
  0.0 49.3 jit_solution(6874440466596179603)
XLA Ops:
  0.0 0.0 copy-start
  0.0 0.7 %copy-done = s32[2,2,256]{2,1,0:T(2,128)S(1)} copy-done((s32[2,2,256]{2,1,0:T(2,128)S(1)}, s32[2,2,256]{2,1,0:T(2,128)}, u32[]{:S(2)}) %copy-start) | copy-done | bytes 4120
  0.7 47.7 %exchange.1 = (f32[4,64,128]{2,1,0:T(8,128)S(1)}, f32[4,16,128]{2,1,0:T(8,128)S(1)}) custom-call(bf16[16,1024,128]{2,1,0:T(8,128)(2,1)} %bitcast.5, bf16[2,1024,1024]{2,1,0:T(8,128)(2,1)} %bitcast.6, s32[2,2,256]{2,1,0:T(2,128)S(1)} %copy-done, s32[16,16,16,64]{3,2,1,0:T(8,128)} %occupation.1), custom_call_target="tpu_custom_call" | custom-call | tf_op jit(solution)/shard_map/exchange/pallas_call | solution.py:222
  48.4 1.0 %multiply_reduce_fusion = f32[16,64,128]{2,1,0:T(8,128)} fusion(f32[4,64,128]{2,1,0:T(8,128)S(1)} %get-tuple-element.8, f32[4,16,128]{2,1,0:T(8,128)S(1)} %get-tuple-element.7), kind=kLoop, calls=%fused_computation | loop fusion | flops 917504 | bytes 688128 | tf_op jit(solution)/shard_map/reduce_sum | solution.py:265
Async XLA Ops:
  0.0 0.7 %copy-start = (s32[2,2,256]{2,1,0:T(2,128)S(1)}, s32[2,2,256]{2,1,0:T(2,128)}, u32[]{:S(2)}) copy-start(s32[2,2,256]{2,1,0:T(2,128)} %plan_table.1) | copy-start | bytes 12292

commit v5 on v4

--- a/solution.py
+++ b/solution.py
@@ -150,11 +150,13 @@
     def stacked(m, low, high):
         return jnp.concatenate([orbital[m, low:high], turned[m, low:high]], axis=0)
 
-    def extend(m, other, sign, low, high):
+    def columns(m, low, high):
+        return lax.dot_general(
+            masked[m, :high], stacked(m, low, high), NT, preferred_element_type=F32
+        )
+
+    def extend(density, other, sign, low, high):
         size = high - low
-        density = lax.dot_general(
-            masked[m, :high], stacked(m, low, high), NT, preferred_element_type=F32
-        )
         real, imag = density[:, :size], density[:, size:]
         wr = weight[0, :high, low:high].astype(F32)
         wi = weight[1, :high, low:high].astype(F32) * sign
@@ -180,8 +182,9 @@
         k, p = 2 * turn, 2 * turn + 1
         prepare(k, low, high)
         prepare(p, low, high)
-        extend(p, k, 1.0, low, high)
-        extend(k, p, -1.0, low, high)
+        ofp, ofk = columns(p, low, high), columns(k, low, high)
+        extend(ofp, k, 1.0, low, high)
+        extend(ofk, p, -1.0, low, high)
 
     low = 0
     for size in UNITS[:-1]:
@@ -203,12 +206,13 @@
             block_copy(m).start()
 
     for m in range(messages):
+        for c in range(pieces):
+            orbital_copy(m, c).wait_send()
+    for m in range(messages):
+        block_copy(m).wait_send()
+    for m in reversed(range(messages)):
         block_copy(m).wait_recv()
         out[m] = returned[m].astype(F32)
-    for m in range(messages):
-        for c in range(pieces):
-            orbital_copy(m, c).wait_send()
-        block_copy(m).wait_send()
 
 
 def on_device(counts, orbitals, kernel, plan, occupation):

time: 49.4 us -> 49 us (level)
  Pallas kernels: 47.7 us -> 47.2 us
where the time goes in v5:
time: 49 us; the launch traced here: 48.9 us
  Pallas kernels  47.2 us (96%)
  other arithmetic  0.95 us (2%)
  local copies, waits for them, and re-layouts  0.69 us (1%)
    pallas_call x1, Pallas kernels, on_device(): pl.pallas_call(functools.partial(exchange_kernel, counts, cells, shifts),...  47.2 us

profile of v5, /device:TPU:32, one launch (start us, length us, event | category | flops | bytes accessed | tf_op | source)
XLA Modules:
  0.0 48.9 jit_solution(15717643224121991000)
XLA Ops:
  0.0 0.0 copy-start
  0.0 0.7 %copy-done = s32[2,2,256]{2,1,0:T(2,128)S(1)} copy-done((s32[2,2,256]{2,1,0:T(2,128)S(1)}, s32[2,2,256]{2,1,0:T(2,128)}, u32[]{:S(2)}) %copy-start) | copy-done | bytes 4120
  0.7 47.2 %exchange.1 = (f32[4,64,128]{2,1,0:T(8,128)S(1)}, f32[4,16,128]{2,1,0:T(8,128)S(1)}) custom-call(bf16[16,1024,128]{2,1,0:T(8,128)(2,1)} %bitcast.5, bf16[2,1024,1024]{2,1,0:T(8,128)(2,1)} %bitcast.6, s32[2,2,256]{2,1,0:T(2,128)S(1)} %copy-done, s32[16,16,16,64]{3,2,1,0:T(8,128)} %occupation.1), custom_call_target="tpu_custom_call" | custom-call | tf_op jit(solution)/shard_map/exchange/pallas_call | solution.py:226
  47.9 1.0 %multiply_reduce_fusion = f32[16,64,128]{2,1,0:T(8,128)} fusion(f32[4,64,128]{2,1,0:T(8,128)S(1)} %get-tuple-element.8, f32[4,16,128]{2,1,0:T(8,128)S(1)} %get-tuple-element.7), kind=kLoop, calls=%fused_computation | loop fusion | flops 917504 | bytes 688128 | tf_op jit(solution)/shard_map/reduce_sum | solution.py:269
Async XLA Ops:
  0.0 0.7 %copy-start = (s32[2,2,256]{2,1,0:T(2,128)S(1)}, s32[2,2,256]{2,1,0:T(2,128)}, u32[]{:S(2)}) copy-start(s32[2,2,256]{2,1,0:T(2,128)} %plan_table.1) | copy-start | bytes 12292

commit v6 on v5

--- a/solution.py
+++ b/solution.py
@@ -64,13 +64,13 @@
             device_id_type=MESH,
         )
 
-    def block_copy(m):
+    def block_copy(m, source=None):
         return pltpu.make_async_remote_copy(
             src_ref=block.at[m],
             dst_ref=returned.at[m],
             send_sem=back_send_sem.at[m],
             recv_sem=back_recv_sem.at[m],
-            device_id=sources[m],
+            device_id=sources[m] if source is None else source,
             device_id_type=MESH,
         )
 
@@ -88,7 +88,7 @@
         pltpu.make_async_copy(orbitals.at[:, rows(c)], local[c], local_sem.at[c])
         for c in range(pieces)
     ]
-    for copy in local_copies:
+    for copy in local_copies[:2]:
         copy.start()
     weight_copy = pltpu.make_async_copy(weights, weight, weight_sem)
     occupied_copies = []
@@ -105,12 +105,12 @@
                 occupied_sem.at[m],
             )
         )
-    for copy in occupied_copies:
-        copy.start()
     plan_copy.wait()
     own_slots = [slot_of(m, places) for m in range(messages)]
     for c in range(pieces):
         local_copies[c].wait()
+        if c + 2 < pieces:
+            local_copies[c + 2].start()
         for m in range(messages):
             sending[m, rows(c)] = local[c][own_slots[m]]
         if c == 0:
@@ -118,6 +118,8 @@
         for m in ORDER:
             orbital_copy(m, c).start()
     weight_copy.start()
+    for copy in occupied_copies:
+        copy.start()
 
     for m in range(messages):
         numbers = lax.broadcasted_iota(jnp.int32, slots.shape[1:], 0)
@@ -196,14 +198,18 @@
 
         low = high
 
-    for turn in reversed(range(turns)):
+    @pl.loop(0, turns)
+    def _(step):
+        turn = turns - 1 - step
         unit(turn, low, nmu)
-        for m in (2 * turn, 2 * turn + 1):
+        forward, partner = hop_shifts(turn, counts)
+        for m, shift in ((2 * turn, forward), (2 * turn + 1, partner)):
             gram = jnp.dot(flipped[m], sums[m].astype(BF16), preferred_element_type=F32)
             real = -(gram[:bands, :bands] + gram[bands:, bands:])
             imag = -(gram[:bands, bands:] - gram[bands:, :bands])
             block[m] = jnp.concatenate([real, imag], axis=1).astype(BF16)
-            block_copy(m).start()
+            source = tuple(lax.rem(p - h + n, n) for p, h, n in zip(places, shift, counts))
+            block_copy(m, source).start()
 
     for m in range(messages):
         for c in range(pieces):

time: 49 us -> 49.1 us (level)
  no operation moved by 1% of the time
where the time goes in v6:
time: 49.1 us; the launch traced here: 48.9 us
  Pallas kernels  47.2 us (96%)
  other arithmetic  0.95 us (2%)
  local copies, waits for them, and re-layouts  0.69 us (1%)
    pallas_call x1, Pallas kernels, on_device(): pl.pallas_call(functools.partial(exchange_kernel, counts, cells, shifts),...  47.2 us

profile of v6, /device:TPU:32, one launch (start us, length us, event | category | flops | bytes accessed | tf_op | source)
XLA Modules:
  0.0 48.9 jit_solution(9536850860303133915)
XLA Ops:
  0.0 0.0 copy-start
  0.0 0.7 %copy-done = s32[2,2,256]{2,1,0:T(2,128)S(1)} copy-done((s32[2,2,256]{2,1,0:T(2,128)S(1)}, s32[2,2,256]{2,1,0:T(2,128)}, u32[]{:S(2)}) %copy-start) | copy-done | bytes 4120
  0.7 47.2 %exchange.1 = (f32[4,64,128]{2,1,0:T(8,128)S(1)}, f32[4,16,128]{2,1,0:T(8,128)S(1)}) custom-call(bf16[16,1024,128]{2,1,0:T(8,128)(2,1)} %bitcast.5, bf16[2,1024,1024]{2,1,0:T(8,128)(2,1)} %bitcast.6, s32[2,2,256]{2,1,0:T(2,128)S(1)} %copy-done, s32[16,16,16,64]{3,2,1,0:T(8,128)} %occupation.1), custom_call_target="tpu_custom_call" | custom-call | tf_op jit(solution)/shard_map/exchange/pallas_call | solution.py:232
  47.9 1.0 %multiply_reduce_fusion = f32[16,64,128]{2,1,0:T(8,128)} fusion(f32[4,64,128]{2,1,0:T(8,128)S(1)} %get-tuple-element.8, f32[4,16,128]{2,1,0:T(8,128)S(1)} %get-tuple-element.7), kind=kLoop, calls=%fused_computation | loop fusion | flops 917504 | bytes 688128 | tf_op jit(solution)/shard_map/reduce_sum | solution.py:275
Async XLA Ops:
  0.0 0.7 %copy-start = (s32[2,2,256]{2,1,0:T(2,128)S(1)}, s32[2,2,256]{2,1,0:T(2,128)}, u32[]{:S(2)}) copy-start(s32[2,2,256]{2,1,0:T(2,128)} %plan_table.1) | copy-start | bytes 12292
